TPU v7x, 32 devices: a whole 2x2x4 slice. The times are simulated.
32 devices in a mesh: dp: 4 (over x, core), fsdp: 2 (over y), ctx: 4 (over z).
Axes of the slice: x: 2, y: 2, z: 4, core: 2. Of those that a mesh axis runs over, the one named last changes fastest.
Arguments:
- box_hidden_states: bfloat16 [8, 2048, 8192], P(('dp', 'fsdp'), 'ctx'), may hold values from -60 to 60
- box_token_positions: int32 [8, 2048], P(('dp', 'fsdp')), may hold values from 0 to 8191, as said below
- document_lengths: int32 [8, 3], P(('dp', 'fsdp')), may hold values from 512 to 7168, as said below
- successors: int32 [8, 2048], P(('dp', 'fsdp'), 'ctx'), may hold values from 0 to 2047, as said below
- fixed_key_matrix: bfloat16 [8192, 1024], P('fsdp'), may hold values from -0.0625 to 0.0625
- adapter_down: bfloat16 [8192, 16], replicated, may hold values from -0.0625 to 0.0625
- adapter_up: bfloat16 [16, 1024], replicated, may hold values from -1.5 to 1.5
- pointer_query_map: bfloat16 [1024, 64], replicated, may hold values from -0.1875 to 0.1875
- pointer_key_map: bfloat16 [1024, 64], replicated, may hold values from -0.1875 to 0.1875
Outputs:
- grad_down: float32 [8192, 16], P('fsdp')
- up_gradient: float32 [16, 1024], replicated
- grad_query: float32 [1024, 64], replicated
- grad_key: float32 [1024, 64], replicated
- mean_loss: float32 [], replicated
Inputs may be any that keep to these rules, and one draw needn't show every extreme that they name: `box_token_positions`: each row is increasing; entries k * 512 to (k + 1) * 512 - 1 lie in positions k * 2048 to (k + 1) * 2048 - 1. `document_lengths`: each row holds multiples of 512 that sum to 8192. `successors`: the index of a box token of the same sequence and the same document as the query; the query itself only where it is the document's only box token or so drawn.
All inputs are finite; a program needn't handle non-finite values.
Results may differ from a plain program's by a relative error of at most 0.012.
The roundings to bfloat16 on the way count: a program that leaves them out, or rounds other values in their place, can miss the bound.
Values may be sent and summed in bfloat16 or wider, within the bound.
A program may use at most 128 MiB of HBM per device.

v0:
```python
import math
import jax
import jax.numpy as jnp
from jax import lax
from jax.sharding import PartitionSpec as P

ADAPTER_SCALE = 0.5


def contract_rows(left, right):
    return lax.dot_general(
        left, right, (((0,), (0,)), ((), ())), preferred_element_type=jnp.float32
    )


def contracted_columns(left, right):
    return lax.dot_general(
        left, right, (((1,), (1,)), ((), ())), preferred_element_type=jnp.float32
    )


def precise_rows(left, right):
    return lax.dot_general(
        left.astype(jnp.float32),
        right,
        (((0,), (0,)), ((), ())),
        precision=lax.Precision.HIGHEST,
        preferred_element_type=jnp.float32,
    )


def precise_columns(left, right):
    return lax.dot_general(
        left,
        right.astype(jnp.float32),
        (((1,), (1,)), ((), ())),
        precision=lax.Precision.HIGHEST,
        preferred_element_type=jnp.float32,
    )


def on_device(
    box_hidden_states,
    box_token_positions,
    document_lengths,
    successors,
    fixed_key_matrix,
    adapter_down,
    adapter_up,
    pointer_query_map,
    pointer_key_map,
):
    hidden_states = box_hidden_states[0]
    count = hidden_states.shape[0]
    groups = lax.axis_size("fsdp")
    seqs_all = lax.axis_size("dp") * groups
    ctx_count = lax.axis_size("ctx")
    width = pointer_query_map.shape[1]
    scale = 1.0 / math.sqrt(width)
    pointer_heads = jnp.concatenate([pointer_query_map, pointer_key_map], axis=1)
    adapter_pointer = jnp.dot(adapter_up, pointer_heads, preferred_element_type=jnp.float32).astype(
        jnp.bfloat16
    )
    complete_keys = lax.all_gather(fixed_key_matrix, "fsdp", axis=0, tiled=True)
    pointer_logits = jnp.dot(
        complete_keys, pointer_heads, preferred_element_type=jnp.float32
    ).astype(jnp.bfloat16)
    projected_states = jnp.dot(hidden_states, pointer_logits, preferred_element_type=jnp.float32)
    narrow_rows = jnp.dot(hidden_states, adapter_down, preferred_element_type=jnp.float32).astype(
        jnp.bfloat16
    )
    blended_terms = (
        projected_states
        + ADAPTER_SCALE * jnp.dot(narrow_rows, adapter_pointer, preferred_element_type=jnp.float32)
    ).astype(jnp.bfloat16)
    queries = blended_terms[:, :width]
    keys = blended_terms[:, width:]
    all_keys = lax.all_gather(keys, "ctx", axis=0, tiled=True)
    ends = jnp.cumsum(document_lengths[0])
    segment = jnp.sum(
        (box_token_positions[0][:, None] >= ends[None, :-1]).astype(jnp.int32), axis=1
    )
    own_segment = lax.dynamic_slice_in_dim(segment, lax.axis_index("ctx") * count, count)
    scores = contracted_columns(queries, all_keys) * scale
    same = own_segment[:, None] == segment[None, :]
    masked = jnp.where(same, scores, -jnp.inf)
    top = jnp.max(masked, axis=1, keepdims=True)
    total = jnp.sum(jnp.exp(masked - top), axis=1, keepdims=True)
    lse = top + jnp.log(total)
    column = jnp.arange(scores.shape[1], dtype=jnp.int32)
    hit = column[None, :] == successors[0][:, None]
    picked = jnp.sum(jnp.where(hit, scores, 0.0), axis=1)
    loss_part = jnp.sum(lse[:, 0] - picked)
    prob = jnp.exp(masked - lse)
    weights = ((prob - hit.astype(jnp.float32)) * (scale * (1.0 / seqs_all))).astype(jnp.bfloat16)
    grad_q = jnp.dot(weights, all_keys, preferred_element_type=jnp.float32).astype(jnp.bfloat16)
    grad_k = lax.psum_scatter(
        contract_rows(weights, queries), "ctx", scatter_dimension=0, tiled=True
    ).astype(jnp.bfloat16)
    paired_terms = jnp.concatenate([grad_q, grad_k], axis=1)
    narrow_gradient = (ADAPTER_SCALE * contracted_columns(paired_terms, adapter_pointer)).astype(
        jnp.bfloat16
    )
    projection_gradient = contract_rows(hidden_states, paired_terms)
    narrow_rows_gradient = contract_rows(narrow_rows, paired_terms)
    grad_down = contract_rows(hidden_states, narrow_gradient)
    denominator = seqs_all * count * ctx_count
    rows_each = grad_down.shape[0] // groups
    summed_terms = lax.psum(
        (grad_down, projection_gradient, narrow_rows_gradient, loss_part), ("dp", "fsdp", "ctx")
    )
    head_gradients = precise_rows(complete_keys, summed_terms[1]) + ADAPTER_SCALE * precise_rows(
        adapter_up, summed_terms[2]
    )
    up_gradient = ADAPTER_SCALE * precise_columns(summed_terms[2], pointer_heads)
    down_rows = lax.dynamic_slice_in_dim(
        summed_terms[0], lax.axis_index("fsdp") * rows_each, rows_each, 0
    )
    return (
        down_rows,
        up_gradient,
        head_gradients[:, :width],
        head_gradients[:, width:],
        summed_terms[3] / denominator,
    )


def solution(mesh):
    in_specs = (
        P(("dp", "fsdp"), "ctx", None),
        P(("dp", "fsdp"), None),
        P(("dp", "fsdp"), None),
        P(("dp", "fsdp"), "ctx"),
        P("fsdp", None),
        P(),
        P(),
        P(),
        P(),
    )
    out_specs = (P("fsdp", None), P(), P(), P(), P())
    return jax.shard_map(
        on_device, mesh=mesh, in_specs=in_specs, out_specs=out_specs, check_vma=False
    )
```

profile of v0, /device:TPU:0, one launch (start us, length us, event | category | flops | bytes accessed | tf_op | source)
XLA Modules:
  0.0 445.7 jit_solution(16629726569500244938)
XLA Ops:
  7.2 0.0 all-gather.2.cloned.1.call-start
  7.3 0.7 all-gather.2.cloned.1.call-update
  8.0 0.0 reduce-scatter.2.cloned.1.call-start
  8.0 0.2 reduce-window.4
  8.2 0.1 fusion.24
  8.3 0.1 dynamic_slice.6
  8.4 0.2 convolution_convert_fusion.2
  8.6 5.7 %fusion.15 = bf16[512,16]{0,1:T(8,128)(2,1)S(1)} fusion(bf16[8192,16]{0,1:T(8,128)(2,1)S(1)} %copy-done, bf16[1,512,8192]{2,1,0:T(8,128)(2,1)} %param.9), kind=kOutput, calls=%fused_computation.26 | convolution fusion | flops 134225920 | bytes 8667136 | tf_op jit(solution)/shard_map/dot_general | solution.py:69
  14.3 196.9 %all-gather.2.cloned.1.call-done = bf16[8192,1024]{1,0:T(8,128)(2,1)} async-done(((bf16[4096,1024]{1,0:T(8,128)(2,1)}), bf16[8192,1024]{1,0:T(8,128)(2,1)}) %all-gather.2.cloned.1.call-update) | async-done | bytes 16777232 | tf_op jit(solution)/shard_map/all_gather | solution.py:64
  211.2 13.1 %fusion.10 = f32[512,128]{0,1:T(8,128)S(1)} fusion(bf16[1,512,8192]{2,1,0:T(8,128)(2,1)} %param.9, bf16[1024,128]{0,1:T(8,128)(2,1)S(1)} %constant_dynamic-update-slice_fusion, bf16[8192,1024]{1,0:T(8,128)(2,1)} %all-gather.2.cloned.1.call-done), kind=kOutput, calls=%fused_computation.21 | convolution fusion | flops 3222274048 | bytes 25690112 | tf_op jit(solution)/shard_map/dot_general | solution.py:68
  224.4 0.2 fusion.13
  224.6 13.9 %all_gather.7 = bf16[2048,64]{0,1:T(8,128)(2,1)S(1)} all-gather(bf16[512,64]{0,1:T(8,128)(2,1)S(1)} %slice.22), channel_id=1, replica_groups=mesh['dp'=4,'fsdp'=2,'ctx'=4] {'ctx'}, dimensions={0}, use_global_device_ids=true | all-gather | bytes 327680 | tf_op jit(solution)/shard_map/all_gather | solution.py:78
  238.6 0.9 fusion.6
  239.4 2.1 select_reduce_fusion
  241.5 0.6 subtract_reduce_fusion
  242.1 1.9 multiply_convert_fusion
  244.0 1.3 fusion.19
  245.3 0.0 reduce-scatter.2.cloned.1.call-update
  245.3 0.2 all-reduce.4.cloned.1.call-start
  245.5 0.8 convolution_convert_fusion.1
  246.3 21.2 %reduce-scatter.2.cloned.1.call-done = f32[512,64]{0,1:T(8,128)} async-done(((f32[2048,64]{0,1:T(8,128)}), f32[512,64]{0,1:T(8,128)}) %reduce-scatter.2.cloned.1.call-update) | async-done | bytes 131088 | tf_op jit(solution)/shard_map/reduce_scatter | solution.py:97
  267.5 0.9 convert_element_type.43
  268.4 5.7 %convolution_bitcast_fusion.1 = f32[8192,16]{0,1:T(8,128)} fusion(bf16[1,512,8192]{2,1,0:T(8,128)(2,1)} %param.9, bf16[128,16]{0,1:T(8,128)(2,1)S(1)} %convolution_convert_fusion.2, bf16[512,64]{0,1:T(8,128)(2,1)S(1)} %convert_element_type.43, bf16[512,64]{0,1:T(8,128)(2,1)S(1)} %convolution_convert_fusion.1), kind=kOutput, calls=%fused_computation.2 | convolution fusion | flops 136593408 | bytes 9048064 | tf_op jit(solution)/shard_map/dot_general | solution.py:11
  274.1 6.6 %convolution_bitcast_fusion = f32[8192,128]{0,1:T(8,128)} fusion(bf16[1,512,8192]{2,1,0:T(8,128)(2,1)} %param.9, bf16[512,64]{0,1:T(8,128)(2,1)S(1)} %convert_element_type.43, bf16[512,64]{0,1:T(8,128)(2,1)S(1)} %convolution_convert_fusion.1), kind=kOutput, calls=%fused_computation | convolution fusion | flops 1074003968 | bytes 12713984 | tf_op jit(solution)/shard_map/dot_general | solution.py:11
  280.8 0.1 fusion.23
  280.9 39.2 %all-reduce = (f32[16,128]{1,0:T(8,128)S(1)}, f32[]{:T(128)}) all-reduce(f32[16,128]{1,0:T(8,128)S(1)} %fusion.23, f32[]{:T(128)} %get-tuple-element.11), channel_id=1, replica_groups=mesh['dp'=4,'fsdp'=2,'ctx'=4] {'dp','fsdp','ctx'}, use_global_device_ids=true, to_apply=%region_6.7 | all-reduce | flops 2049 | bytes 16392 | tf_op jit(solution)/shard_map/psum | solution.py:109
  320.7 0.9 convolution_multiply_fusion.3
  321.6 102.4 %all-reduce.4.cloned.1.call-done = (f32[8192,16]{0,1:T(8,128)}, f32[8192,128]{0,1:T(8,128)}) async-done(((f32[8192,16]{0,1:T(8,128)}, f32[8192,128]{0,1:T(8,128)}), (f32[8192,16]{0,1:T(8,128)}, f32[8192,128]{0,1:T(8,128)})) %all-reduce.4.cloned.1.call-update) | async-done | bytes 4718608 | tf_op jit(solution)/shard_map/psum | solution.py:109
  424.0 12.0 %fusion.31 = f32[128,1024]{1,0:T(8,128)S(1)} fusion(f32[8192,128]{0,1:T(8,128)} %get-tuple-element.10, bf16[8192,1024]{1,0:T(8,128)(2,1)} %all-gather.2.cloned.1.call-done), kind=kOutput, calls=%fused_computation.48 | convolution fusion | flops 12884901888 | bytes 21495808 | tf_op jit(solution)/shard_map/dot_general | solution.py:23
  436.1 0.4 fusion.8
  436.5 0.8 fusion.30
  437.3 0.7 constant_dynamic-slice_fusion
  (21 shorter events, 0.1 us)
Async XLA Ops:
  7.2 1.5 copy-start
  7.2 0.8 copy-start.7
  7.2 1.0 copy-start.6
  7.2 1.2 copy-start.3
  7.2 1.2 copy-start.4
  7.2 1.2 copy-start.1
  7.2 204.0 %all-gather.2.cloned.1.call-start = ((), (), s32[]{:S(2)}) async-start(), calls=%async_computation.1 | async-start | bytes 25165824 | tf_op jit(solution)/shard_map/all_gather | solution.py:64
  8.0 259.6 %reduce-scatter.2.cloned.1.call-start = ((), (), s32[]{:S(2)}) async-start(), calls=%async_computation.2 | async-start | bytes 655360 | tf_op jit(solution)/shard_map/reduce_scatter | solution.py:97
  224.4 15.1 %copy-start.5 = (s32[1,512]{1,0:T(1,128)S(1)}, s32[1,512]{1,0:T(1,128)}, u32[]{:S(2)}) copy-start(s32[1,512]{1,0:T(1,128)} %param.12) | copy-start | bytes 6148
  245.3 178.7 %all-reduce.4.cloned.1.call-start = ((), (), s32[]{:S(2)}) async-start(), calls=%async_computation.3 | async-start | bytes 9437184 | tf_op jit(solution)/shard_map/psum | solution.py:109
  424.0 13.3 %copy-start.2 = (f32[8192,16]{0,1:T(8,128)S(1)}, f32[8192,16]{0,1:T(8,128)}, u32[]{:S(2)}) copy-start(f32[8192,16]{0,1:T(8,128)} %get-tuple-element.9) | copy-start | bytes 1572868
Sparse Core Ops, SparseCore 0:
  9.6 201.5 all-gather.1
  245.4 22.0 reduce-scatter.1
  280.9 143.0 all-reduce.3
where the time goes:
time: 446 us
  waiting for transfers between devices  321 us (72%)
  blocking collectives  53.1 us (12%)
  matrix products  47.9 us (11%)
  between operations  15.7 us (4%)
  other arithmetic  5.73 us (1%)
    all_gather x1, waiting for transfers between devices, on_device(): complete_keys = lax.all_gather(fixed_key_matrix, 'fsdp', axis=0, tiled=True)  197 us
    psum x1, waiting for transfers between devices, on_device(): lax.psum((grad_down, projection_gradient, narrow_rows_gradient, loss_part...  102 us
    psum x1, blocking collectives, on_device(): lax.psum((grad_down, projection_gradient, narrow_rows_gradient, loss_part...  39.2 us
    reduce_scatter x1, waiting for transfers between devices, on_device(): lax.psum_scatter(contract_rows(weights, queries), 'ctx', scatter_dimensio...  21.2 us
    all_gather x1, blocking collectives, on_device(): all_keys = lax.all_gather(keys, 'ctx', axis=0, tiled=True)  13.9 us
    dot_general x4, matrix products, contract_rows(): lax.dot_general(left, right, (((0,), (0,)), ((), ())), preferred_element_...  13.7 us
    dot_general x1, matrix products, on_device(): jnp.dot(hidden_states, pointer_logits, preferred_element_type=jnp.float32)  13.1 us
    dot_general x2, matrix products, precise_rows(): lax.dot_general(left.astype(jnp.float32), right, (((0,), (0,)), ((), ()))...  12.5 us
  transfers between devices with their start and end apart: 3, of which 3 were waited for; matrix products, arithmetic and copies ran while one was open for 2% of the time, Pallas kernels for 0%

commit v1 on v0

--- a/solution.py
+++ b/solution.py
@@ -107,7 +107,10 @@
     denominator = seqs_all * count * ctx_count
     rows_each = grad_down.shape[0] // groups
     summed_terms = lax.psum(
-        (grad_down, projection_gradient, narrow_rows_gradient, loss_part), ("dp", "fsdp", "ctx")
+        lax.psum(
+            (grad_down, projection_gradient, narrow_rows_gradient, loss_part), ("fsdp", "ctx")
+        ),
+        "dp",
     )
     head_gradients = precise_rows(complete_keys, summed_terms[1]) + ADAPTER_SCALE * precise_rows(
         adapter_up, summed_terms[2]

time: 446 us -> 567 us (1.27)
  waiting for transfers between devices: 321 us -> 453 us
  blocking collectives: 53.1 us -> 42.4 us
    psum x1, waiting for transfers between devices: 102 us -> 168 us  [on_device(): lax.psum((grad_down, projection_gradient, narrow_rows_gradient, loss_part...]
    psum x0 -> x1, waiting for transfers between devices: none -> 65.7 us  [on_device(): lax.psum(lax.psum((grad_down, projection_gradient, narrow_rows_gradient,...]
    psum x1, blocking collectives: 39.2 us -> 20.7 us  [on_device(): lax.psum((grad_down, projection_gradient, narrow_rows_gradient, loss_part...]
    psum x0 -> x1, blocking collectives: none -> 7.75 us  [on_device(): lax.psum(lax.psum((grad_down, projection_gradient, narrow_rows_gradient,...]
  transfers between devices with their start and end apart: 3 -> 4, of which waited for: 3 -> 4; matrix products, arithmetic and copies ran while one was open for 2% -> 1% of each run, Pallas kernels for 0% -> 0%
where the time goes in v1:
time: 567 us
  waiting for transfers between devices  453 us (80%)
  matrix products  47.8 us (8%)
  blocking collectives  42.4 us (7%)
  between operations  15.7 us (3%)
  other arithmetic  5.73 us (1%)
    all_gather x1, waiting for transfers between devices, on_device(): complete_keys = lax.all_gather(fixed_key_matrix, 'fsdp', axis=0, tiled=True)  197 us
    psum x1, waiting for transfers between devices, on_device(): lax.psum((grad_down, projection_gradient, narrow_rows_gradient, loss_part...  168 us
    psum x1, waiting for transfers between devices, on_device(): lax.psum(lax.psum((grad_down, projection_gradient, narrow_rows_gradient,...  65.7 us
    reduce_scatter x1, waiting for transfers between devices, on_device(): lax.psum_scatter(contract_rows(weights, queries), 'ctx', scatter_dimensio...  21.4 us
    psum x1, blocking collectives, on_device(): lax.psum((grad_down, projection_gradient, narrow_rows_gradient, loss_part...  20.7 us
    all_gather x1, blocking collectives, on_device(): all_keys = lax.all_gather(keys, 'ctx', axis=0, tiled=True)  13.9 us
    dot_general x4, matrix products, contract_rows(): lax.dot_general(left, right, (((0,), (0,)), ((), ())), preferred_element_...  13.7 us
    dot_general x1, matrix products, on_device(): jnp.dot(hidden_states, pointer_logits, preferred_element_type=jnp.float32)  13.1 us
  transfers between devices with their start and end apart: 4, of which 4 were waited for; matrix products, arithmetic and copies ran while one was open for 1% of the time, Pallas kernels for 0%

profile of v1, /device:TPU:0, one launch (start us, length us, event | category | flops | bytes accessed | tf_op | source)
XLA Modules:
  0.0 566.8 jit_solution(10824941121797738169)
XLA Ops:
  7.3 0.7 all-gather.2.cloned.1.call-update
  8.0 0.2 reduce-window.4
  8.2 0.1 fusion.24
  8.3 0.1 dynamic_slice.6
  8.4 0.2 convolution_convert_fusion.2
  8.6 5.7 fusion.15
  14.3 196.9 %all-gather.2.cloned.1.call-done = bf16[8192,1024]{1,0:T(8,128)(2,1)} async-done(((bf16[4096,1024]{1,0:T(8,128)(2,1)}), bf16[8192,1024]{1,0:T(8,128)(2,1)}) %all-gather.2.cloned.1.call-update) | async-done | bytes 16777232 | tf_op jit(solution)/shard_map/all_gather | solution.py:64
  211.2 13.1 %fusion.10 = f32[512,128]{0,1:T(8,128)S(1)} fusion(bf16[1,512,8192]{2,1,0:T(8,128)(2,1)} %param.9, bf16[1024,128]{0,1:T(8,128)(2,1)S(1)} %constant_dynamic-update-slice_fusion, bf16[8192,1024]{1,0:T(8,128)(2,1)} %all-gather.2.cloned.1.call-done), kind=kOutput, calls=%fused_computation.21 | convolution fusion | flops 3222274048 | bytes 25690112 | tf_op jit(solution)/shard_map/dot_general | solution.py:68
  224.4 0.2 fusion.13
  224.6 13.9 %all_gather.7 = bf16[2048,64]{0,1:T(8,128)(2,1)S(1)} all-gather(bf16[512,64]{0,1:T(8,128)(2,1)S(1)} %slice.22), channel_id=1, replica_groups=mesh['dp'=4,'fsdp'=2,'ctx'=4] {'ctx'}, dimensions={0}, use_global_device_ids=true | all-gather | bytes 327680 | tf_op jit(solution)/shard_map/all_gather | solution.py:78
  238.6 0.9 fusion.6
  239.4 2.1 select_reduce_fusion
  241.5 0.6 subtract_reduce_fusion
  242.1 1.9 multiply_convert_fusion
  244.0 1.3 fusion.19
  245.3 0.0 all-reduce.7.cloned.1.call-start
  245.3 0.8 convolution_convert_fusion.1
  246.1 21.4 %reduce-scatter.2.cloned.1.call-done = f32[512,64]{0,1:T(8,128)} async-done(((f32[2048,64]{0,1:T(8,128)}), f32[512,64]{0,1:T(8,128)}) %reduce-scatter.2.cloned.1.call-update) | async-done | bytes 131088 | tf_op jit(solution)/shard_map/reduce_scatter | solution.py:97
  267.5 0.9 convert_element_type.43
  268.5 5.7 %convolution_bitcast_fusion.1 = f32[8192,16]{0,1:T(8,128)} fusion(bf16[1,512,8192]{2,1,0:T(8,128)(2,1)} %param.9, bf16[128,16]{0,1:T(8,128)(2,1)S(1)} %convolution_convert_fusion.2, bf16[512,64]{0,1:T(8,128)(2,1)S(1)} %convert_element_type.43, bf16[512,64]{0,1:T(8,128)(2,1)S(1)} %convolution_convert_fusion.1), kind=kOutput, calls=%fused_computation.2 | convolution fusion | flops 136593408 | bytes 9048064 | tf_op jit(solution)/shard_map/dot_general | solution.py:11
  274.2 6.6 %convolution_bitcast_fusion = f32[8192,128]{0,1:T(8,128)} fusion(bf16[1,512,8192]{2,1,0:T(8,128)(2,1)} %param.9, bf16[512,64]{0,1:T(8,128)(2,1)S(1)} %convert_element_type.43, bf16[512,64]{0,1:T(8,128)(2,1)S(1)} %convolution_convert_fusion.1), kind=kOutput, calls=%fused_computation | convolution fusion | flops 1074003968 | bytes 12713984 | tf_op jit(solution)/shard_map/dot_general | solution.py:11
  280.8 0.2 all-reduce.9.cloned.1.call-start
  281.0 168.3 %all-reduce.7.cloned.1.call-done = (f32[8192,16]{0,1:T(8,128)}, f32[8192,128]{0,1:T(8,128)}) async-done(((f32[8192,16]{0,1:T(8,128)}, f32[8192,128]{0,1:T(8,128)}), (f32[8192,16]{0,1:T(8,128)}, f32[8192,128]{0,1:T(8,128)})) %all-reduce.7.cloned.1.call-update) | async-done | bytes 4718608 | tf_op jit(solution)/shard_map/psum | solution.py:110
  449.3 0.1 fusion.23
  449.5 20.7 %all-reduce = (f32[16,128]{1,0:T(8,128)S(1)}, f32[]{:T(128)}) all-reduce(f32[16,128]{1,0:T(8,128)S(1)} %fusion.23, f32[]{:T(128)} %get-tuple-element.15), channel_id=1, replica_groups=mesh['dp'=4,'fsdp'=2,'ctx'=4] {'fsdp','ctx'}, use_global_device_ids=true, to_apply=%region_7.8 | all-reduce | flops 2049 | bytes 16392 | tf_op jit(solution)/shard_map/psum | solution.py:110
  470.2 7.8 %all-reduce.2 = (f32[16,128]{1,0:T(8,128)S(1)}, f32[]{:T(128)}) all-reduce(f32[16,128]{1,0:T(8,128)S(1)} %get-tuple-element.7, f32[]{:T(128)} %get-tuple-element.8), channel_id=1, replica_groups=mesh['dp'=4,'fsdp'=2,'ctx'=4] {'dp'}, use_global_device_ids=true, to_apply=%region_8.9 | all-reduce | flops 2049 | bytes 16392 | tf_op jit(solution)/shard_map/psum | solution.py:109
  478.6 0.9 convolution_multiply_fusion.3
  479.5 65.7 %all-reduce.9.cloned.1.call-done = (f32[8192,16]{0,1:T(8,128)}, f32[8192,128]{0,1:T(8,128)}) async-done(((f32[8192,16]{0,1:T(8,128)}, f32[8192,128]{0,1:T(8,128)}), (f32[8192,16]{0,1:T(8,128)}, f32[8192,128]{0,1:T(8,128)})) %all-reduce.9.cloned.1.call-update) | async-done | bytes 4718608 | tf_op jit(solution)/shard_map/psum | solution.py:109
  545.2 12.0 %fusion.31 = f32[128,1024]{1,0:T(8,128)S(1)} fusion(f32[8192,128]{0,1:T(8,128)} %get-tuple-element.14, bf16[8192,1024]{1,0:T(8,128)(2,1)} %all-gather.2.cloned.1.call-done), kind=kOutput, calls=%fused_computation.48 | convolution fusion | flops 12884901888 | bytes 21495808 | tf_op jit(solution)/shard_map/dot_general | solution.py:23
  557.2 0.4 fusion.8
  557.6 0.8 fusion.30
  558.4 0.7 constant_dynamic-slice_fusion
  (25 shorter events, 0.2 us)
Async XLA Ops:
  7.2 1.5 copy-start
  7.2 0.8 copy-start.7
  7.2 1.0 copy-start.6
  7.2 1.2 copy-start.3
  7.2 1.2 copy-start.4
  7.2 1.2 copy-start.1
  7.2 204.0 %all-gather.2.cloned.1.call-start = ((), (), s32[]{:S(2)}) async-start(), calls=%async_computation.1 | async-start | bytes 25165824 | tf_op jit(solution)/shard_map/all_gather | solution.py:64
  8.0 259.6 %reduce-scatter.2.cloned.1.call-start = ((), (), s32[]{:S(2)}) async-start(), calls=%async_computation.2 | async-start | bytes 655360 | tf_op jit(solution)/shard_map/reduce_scatter | solution.py:97
  224.4 15.1 %copy-start.5 = (s32[1,512]{1,0:T(1,128)S(1)}, s32[1,512]{1,0:T(1,128)}, u32[]{:S(2)}) copy-start(s32[1,512]{1,0:T(1,128)} %param.12) | copy-start | bytes 6148
  245.3 204.0 %all-reduce.7.cloned.1.call-start = ((), (), s32[]{:S(2)}) async-start(), calls=%async_computation.3 | async-start | bytes 9437184 | tf_op jit(solution)/shard_map/psum | solution.py:110
  280.8 264.4 %all-reduce.9.cloned.1.call-start = ((), (), s32[]{:S(2)}) async-start(), calls=%async_computation.4 | async-start | bytes 9437184 | tf_op jit(solution)/shard_map/psum | solution.py:109
  545.2 13.3 %copy-start.2 = (f32[8192,16]{0,1:T(8,128)S(1)}, f32[8192,16]{0,1:T(8,128)}, u32[]{:S(2)}) copy-start(f32[8192,16]{0,1:T(8,128)} %get-tuple-element.13) | copy-start | bytes 1572868
Sparse Core Ops, SparseCore 0:
  9.6 201.5 all-gather.1
  245.4 22.0 reduce-scatter.1
  280.9 168.3 all-reduce.6
  451.6 93.5 all-reduce.8
